TPU v7x, 32 devices: a whole 2x2x4 slice. The times are simulated.
32 devices in a mesh: mapx: 8 (over z, x), mapy: 2 (over y), layer: 2 (over core).
Axes of the slice: x: 2, y: 2, z: 4, core: 2. Of those that a mesh axis runs over, the one named last changes fastest.
Arguments:
- old_state: float32 [8, 2, 2, 6, 8192], P('mapx', 'mapy', 'layer'), as said below
- send_blocks: int32 [8, 2, 2, 10, 16], P('mapx', 'mapy', 'layer'), may hold values from 0 to 63
- node_slots: int32 [8, 2, 2, 4, 512], P('mapx', 'mapy', 'layer'), may hold values from 0 to 20479, as said below
- node_weights: float32 [8, 2, 2, 4, 512], P('mapx', 'mapy', 'layer'), as said below
- front_mask: int32 [8, 2, 2, 512], P('mapx', 'mapy', 'layer'), may hold values 0 or 1
- halo_lists: int32 [8, 2, 2, 6, 256], P('mapx', 'mapy', 'layer'), may hold values from 0 to 511
- elem_nodes: int32 [8, 2, 2, 4, 2560], P('mapx', 'mapy', 'layer'), may hold values from 0 to 2047
- shape_grads: float32 [8, 2, 2, 12, 2560], P('mapx', 'mapy', 'layer'), as said below
- elem_volume: float32 [8, 2, 2, 2560], P('mapx', 'mapy', 'layer'), may hold values from 0.5 to 2
Outputs:
- new_state: float32 [8, 2, 2, 6, 512], P('mapx', 'mapy', 'layer')
- residual: float32 [8, 2, 2, 4, 512], P('mapx', 'mapy', 'layer')
Inputs may be any that keep to these rules, and one draw needn't show every extreme that they name: `send_blocks`: each entry names one of the sender's old blocks; a block may go to several peers or twice to one. `node_slots`: indexes the received nodes, ordered by source (mapx offset plus 2, times 2, plus layer index), then slot, then node in the block; only sources inside the device grid are named. `node_weights`: Positive; the four weights of a node sum to one. `halo_lists`: owned nodes kept as ghosts by the neighbour in direction k. `elem_nodes`: local numbering: the owned nodes first, then 256 ghosts for each of the six directions in order. `shape_grads`: the four gradients of an element sum to zero. `old_state`: rows 0 to 3 velocity and pressure, row 4 temperature in [-1, 0], row 5 damage in [0, 0.9].
All inputs are finite; a program needn't handle non-finite values. No bound on the sum of `front_mask` on one device may be relied on, other than what follows from the above.
Results may differ from a plain program's by a relative error of at most 0.00002.
Values sent between devices are 32-bit elements; how exact they have to be, the bound alone decides.
No kernel may reach another device: no remote copies, remote signals or barrier semaphores. Data moves between devices by JAX's collectives and lax.ppermute only.
A program may use at most 64 MiB of HBM per device.

v0:
```python
import functools

import jax
import jax.numpy as jnp
from jax import lax
from jax.experimental import pallas as pl
from jax.experimental.pallas import tpu as pltpu
from jax.sharding import PartitionSpec as P

BLOCK = 128
REACH = 2
FIELDS = 6
SPLITS = 3

ocean_temp = 0.0
strain_reg = 0.01
gravity = 0.5

AXES = ("mapx", "mapy", "layer")
VMEM = pl.BlockSpec(memory_space=pltpu.VMEM)
SMEM = pl.BlockSpec(memory_space=pltpu.SMEM)


def params():
    return pltpu.CompilerParams(vmem_limit_bytes=32 * 1024 * 1024)


def both_ways(pairs):
    return [way for one, other in pairs for way in ((one, other), (other, one))]


def column_moves(count):
    return [
        both_ways([(at, at + 1) for at in range(1, count - 1, 2)]),
        both_ways([(at + i, at + i + 2) for at in range(0, count - 3, 4) for i in range(2)]),
        both_ways([(at + i, at + i + 2) for at in range(2, count - 3, 4) for i in range(2)]),
        both_ways([(at, at + 1) for at in range(0, count - 1, 2)]),
    ]


def column_offsets():
    at = lax.axis_index("mapx")
    near = jnp.where(lax.rem(at, 2) == 0, 1, -1)
    two = jnp.where(lax.rem(at, 4) < 2, 2, -2)
    return [-near, two, -two, near, 0]


def pair_swap(value, axis, count, first):
    return lax.ppermute(value, axis, both_ways([(at, at + 1) for at in range(first, count - 1, 2)]))


def swap_all(values, sizes):
    long = [axis for axis in range(3) if sizes[axis] > 2]
    steps = [(axis, 1) for axis in long] + [(axis, 0) for axis in range(3)]
    return [pair_swap(value, AXES[axis], sizes[axis], first) for value, (axis, first) in zip(values, steps)]


def pack_kernel(count, *refs):
    blocks_in_ref, old_in_ref = refs[:2]
    cross_ref, mine_ref = refs[2 + count : 4 + count]
    blocks_ref, old_ref, sems = refs[4 + 2 * count :]
    first = [pltpu.make_async_copy(blocks_in_ref, blocks_ref, sems.at[0])]
    first += [pltpu.make_async_copy(old_in_ref, old_ref, sems.at[1])]
    rest = [
        pltpu.make_async_copy(refs[2 + i], refs[4 + count + i], sems.at[2 + i]) for i in range(count)
    ]
    for copy in first + rest:
        copy.start()
    for copy in first:
        copy.wait()
    slots = blocks_ref.shape[2]
    stride = old_ref.shape[0] // FIELDS
    layer = lax.axis_index("layer")
    offsets = column_offsets()
    for out_ref, to_layer in ((cross_ref, 1 - layer), (mine_ref, layer)):
        for q, offset in enumerate(offsets):
            peer = (offset + REACH) * 2 + to_layer
            for c in range(slots):
                rows = pl.ds(blocks_ref[peer, 0, c], FIELDS, stride=stride)
                out_ref[q, FIELDS * c : FIELDS * (c + 1), :] = old_ref[rows, :]
    for copy in rest:
        copy.wait()


def pick(row, lanes):
    return jnp.take_along_axis(jnp.broadcast_to(row, lanes.shape), lanes, axis=1)


def pick_fields(table_ref, block_count, blocks, lanes):
    found = [jnp.zeros((8, BLOCK), jnp.float32) for _ in range(FIELDS)]
    for b in range(block_count):
        hit = blocks == b
        for f in range(FIELDS):
            row = table_ref[b // 2, 2 * f + b % 2 : 2 * f + b % 2 + 1, :]
            found[f] = jnp.where(hit, pick(row, lanes), found[f])
    return found


def add_blocks(ref, chunk, first_block, blocks, lanes, found):
    local = blocks - first_block
    found = list(found)
    for c in range(ref.shape[1] // FIELDS):
        hit = local == c
        for f in range(FIELDS):
            row = ref[chunk, FIELDS * c + f : FIELDS * c + f + 1, :]
            found[f] = jnp.where(hit, pick(row, lanes), found[f])
    return tuple(found)


def first_block(offset, other_layer, slots):
    layer = lax.axis_index("layer")
    return ((offset + REACH) * 2 + (1 - layer if other_layer else layer)) * slots


def cut_rows(from_ref, to_ref):
    count = from_ref.shape[1] // BLOCK
    for r in range(from_ref.shape[0]):
        for i in range(count):
            to_ref[r * count + i : r * count + i + 1, :] = from_ref[r : r + 1, i * BLOCK : (i + 1) * BLOCK]


def near_kernel(
    mine_ref, swap_ref, next_ref, slots_in_ref, weights_in_ref, halos_in_ref, found_ref, slots_ref, weights_ref, halos_ref
):
    for k in range(halos_in_ref.shape[0]):
        cut_rows(halos_in_ref.at[k], halos_ref.at[2 * k : 2 * k + 2])
    cut_rows(slots_in_ref, slots_ref)
    cut_rows(weights_in_ref, weights_ref)
    slots = mine_ref.shape[1] // FIELDS
    offsets = column_offsets()
    for v in range(slots_ref.shape[0] // 8):
        ids = slots_ref[8 * v : 8 * v + 8, :]
        blocks, lanes = ids >> 7, ids & (BLOCK - 1)
        found = tuple(jnp.zeros((8, BLOCK), jnp.float32) for _ in range(FIELDS))
        for ref, chunk, q, other in ((mine_ref, 4, 4, 0), (swap_ref, 4, 4, 1), (next_ref, 0, 0, 0), (next_ref, 1, 0, 1)):
            found = add_blocks(ref, chunk, first_block(offsets[q], other, slots), blocks, lanes, found)
        for f in range(FIELDS):
            found_ref[f, 8 * v : 8 * v + 8, :] = found[f]


def state_kernel(
    counts, two_ref, across_ref, pair_ref, slots_ref, found_ref, weights_ref, mask_ref, halos_ref, state_ref, table_ref, *more_refs
):
    send_refs, cut_ref = more_refs[:-1], more_refs[-1]
    slots = two_ref.shape[1] // FIELDS
    offsets = column_offsets()
    parts = slots_ref.shape[0] // 8
    found = []
    for v in range(parts):
        ids = slots_ref[8 * v : 8 * v + 8, :]
        blocks, lanes = ids >> 7, ids & (BLOCK - 1)
        fields = tuple(found_ref[f, 8 * v : 8 * v + 8, :] for f in range(FIELDS))
        for q, ref in ((1, two_ref), (2, across_ref), (3, pair_ref)):
            for other in range(2):
                fields = add_blocks(ref, other, first_block(offsets[q], other, slots), blocks, lanes, fields)
        found.append(fields)
    front = mask_ref[...] == 1
    rows = mask_ref.shape[0]
    for f in range(FIELDS):
        total = jnp.zeros((rows, BLOCK), jnp.float32)
        for v in range(parts):
            term = found[v][f] * weights_ref[8 * v : 8 * v + 8, :]
            for k in range(8 // rows):
                total = total + term[k * rows : (k + 1) * rows, :]
        if f == 4:
            total = jnp.where(front, ocean_temp, total)
        for r in range(rows):
            state_ref[f : f + 1, r * BLOCK : (r + 1) * BLOCK] = total[r : r + 1, :]
        for s in range(rows // 2):
            table_ref[s, 2 * f : 2 * f + 2, :] = total[2 * s : 2 * s + 2, :]
    starts = (0, halos_ref.shape[0] - 8)
    halo = [halos_ref[first : first + 8, :] for first in starts]
    halo_blocks = [i >> 7 for i in halo]
    halo_lanes = [i & (BLOCK - 1) for i in halo]
    for v in range(2):
        cut = pick_fields(table_ref, rows, halo_blocks[v], halo_lanes[v])
        for k in range(6):
            r = 2 * k - starts[v]
            if 0 <= r <= 6:
                for f in range(FIELDS):
                    cut_ref[k, 2 * f : 2 * f + 2, :] = cut[f][r : r + 2, :]
    send_pairs(counts, cut_ref, send_refs, [(0, 1), (2, 3), (4, 5)])


def pair_places():
    return [lax.rem(lax.axis_index(axis), 2) for axis in AXES]


def send_pairs(counts, cut_ref, send_refs, order):
    places = pair_places()
    long = [axis for axis in range(3) if counts[axis] > 2]
    for axis in range(3):
        even, odd = order[axis]
        send_refs[len(long) + axis][...] = cut_ref[jnp.where(places[axis] == 0, even, odd)]
        if axis in long:
            send_refs[long.index(axis)][...] = cut_ref[jnp.where(places[axis] == 0, odd, even)]


def arrivals(counts, came_refs):
    places = pair_places()
    long = [axis for axis in range(3) if counts[axis] > 2]
    result = []
    for axis in range(3):
        inside = came_refs[len(long) + axis][...]
        at = lax.axis_index(AXES[axis])
        edge = jnp.where(places[axis] == 0, at == 0, at == counts[axis] - 1)
        outside = jnp.zeros_like(inside)
        if axis in long:
            outside = jnp.where(edge, 0.0, came_refs[long.index(axis)][...])
        result.append((places[axis], inside, outside))
    return result


def one_hot_sum(values, ids, block_count):
    rows = lax.broadcasted_iota(jnp.int32, (block_count, BLOCK), 0)
    hit = rows == jnp.broadcast_to(ids >> 7, rows.shape)
    left = [jnp.where(hit, jnp.broadcast_to(v, rows.shape), 0.0) for v in values]
    left = jnp.concatenate(left, axis=0).astype(jnp.bfloat16)
    lanes = lax.broadcasted_iota(jnp.int32, (BLOCK, BLOCK), 0)
    right = jnp.where(lanes == jnp.broadcast_to(ids & (BLOCK - 1), lanes.shape), 1.0, 0.0).astype(jnp.bfloat16)
    return left, right


def cut_parts(value):
    parts = []
    for _ in range(SPLITS - 1):
        part = value.astype(jnp.bfloat16).astype(jnp.float32)
        parts.append(part)
        value = value - part
    return parts + [value]


def nt_dot(left, right):
    return lax.dot_general(left, right, (((1,), (1,)), ((), ())), preferred_element_type=jnp.float32)


def element_kernel(counts, moves, *refs):
    table_in_ref, nodes_in_ref, grads_ref, volume_in_ref = refs[:4]
    came_refs = refs[4 : 4 + moves]
    own_ref = refs[4 + moves]
    send_refs = refs[5 + moves : 5 + 2 * moves]
    table_ref, nodes_ref, volume_ref, values_ref, parts_ref, cut_ref = refs[5 + 2 * moves :]
    owned_slots = table_in_ref.shape[0]
    table_ref[0:owned_slots] = table_in_ref[...]
    for axis, (place_at, inside, outside) in enumerate(arrivals(counts, came_refs)):
        table_ref[owned_slots + 2 * axis + 1 - place_at] = inside
        table_ref[owned_slots + 2 * axis + place_at] = outside
    cut_rows(nodes_in_ref, nodes_ref)
    cut_rows(volume_in_ref, volume_ref)
    block_count = 2 * table_ref.shape[0]
    all_rows = nodes_ref.shape[0]
    elem_rows = all_rows // 4
    for first in range(0, all_rows, 8):
        ids = nodes_ref[first : first + 8, :]
        found = pick_fields(table_ref, block_count, ids >> 7, ids & (BLOCK - 1))
        for f in range(FIELDS):
            values_ref[f, first : first + 8, :] = found[f]
    for first in [*range(0, elem_rows - 7, 8)] + ([elem_rows - 8] if elem_rows % 8 else []):
        at = [slice(r * elem_rows + first, r * elem_rows + first + 8) for r in range(12)]
        values = [[values_ref[f, at[a], :] for f in range(FIELDS)] for a in range(4)]
        grads = [[grads_ref[at[3 * a + j], :] for j in range(3)] for a in range(4)]
        volume = volume_ref[at[0], :]
        velgrad = [[sum(values[a][i] * grads[a][j] for a in range(4)) for j in range(3)] for i in range(3)]
        strain = [[0.5 * (velgrad[i][j] + velgrad[j][i]) if i <= j else None for j in range(3)] for i in range(3)]
        diagonal = sum(strain[i][i] * strain[i][i] for i in range(3))
        corner = sum(strain[i][j] * strain[i][j] for i, j in ((0, 1), (0, 2), (1, 2)))
        second = 0.5 * diagonal + corner
        pressure, temper, damage = [0.25 * (values[0][f] + values[1][f] + values[2][f] + values[3][f]) for f in (3, 4, 5)]
        root = jnp.exp(jnp.log(second + strain_reg) * (-1.0 / 3.0))
        twice = (1.0 - damage) * jnp.exp(-temper) * root
        stress = [[None] * 3 for _ in range(3)]
        for i in range(3):
            for j in range(i, 3):
                stress[i][j] = twice * strain[i][j] - (pressure if i == j else 0.0)
                stress[j][i] = stress[i][j]
        lift = (0.25 * gravity) * volume
        flow = 0.25 * volume * (velgrad[0][0] + velgrad[1][1] + velgrad[2][2])
        for s, part in enumerate(cut_parts(flow)):
            for a in range(4):
                parts_ref[3 * SPLITS + s, at[a], :] = part
        for a in range(4):
            for i in range(3):
                force = volume * sum(stress[i][j] * grads[a][j] for j in range(3))
                if i == 2:
                    force = force + lift
                for s, part in enumerate(cut_parts(force)):
                    parts_ref[i * SPLITS + s, at[a], :] = part

    group = 10

    def gather_terms(step, total):
        lefts, rights = [], []
        for r in range(group):
            at = pl.ds(step * group + r, 1)
            terms = [parts_ref[c * SPLITS + s, at, :] for s in range(SPLITS) for c in range(4)]
            left, right = one_hot_sum(terms, nodes_ref[at, :], block_count)
            lefts.append(left)
            rights.append(right)
        return total + nt_dot(jnp.concatenate(lefts, axis=1), jnp.concatenate(rights, axis=1))

    width = 4 * block_count
    total = lax.fori_loop(0, all_rows // group, gather_terms, jnp.zeros((SPLITS * width, BLOCK), jnp.float32))
    total = sum(total[s * width : (s + 1) * width, :] for s in range(SPLITS))
    owned = 2 * owned_slots
    for c in range(4):
        own_ref[c * owned : (c + 1) * owned, :] = total[c * block_count : c * block_count + owned, :]
        for k in range(6):
            first = c * block_count + owned + 2 * k
            cut_ref[k, 2 * c : 2 * c + 2, :] = total[first : first + 2, :]
    send_pairs(counts, cut_ref, send_refs, [(1, 0), (3, 2), (5, 4)])


def residual_kernel(counts, moves, *refs):
    own_ref, halos_ref = refs[:2]
    out_ref, came_ref = refs[2 + moves :]
    for axis, (place_at, inside, outside) in enumerate(arrivals(counts, refs[2 : 2 + moves])):
        came_ref[2 * axis + place_at] = inside
        came_ref[2 * axis + 1 - place_at] = outside
    owned = own_ref.shape[0] // 4
    lefts, rights = [], []
    for k in range(6):
        parts = cut_parts(came_ref[k])
        for h in range(2):
            ids = halos_ref[2 * k + h : 2 * k + h + 1, :]
            terms = [parts[s][2 * c + h : 2 * c + h + 1, :] for s in range(SPLITS) for c in range(4)]
            left, right = one_hot_sum(terms, ids, owned)
            lefts.append(left)
            rights.append(right)
    total = nt_dot(jnp.concatenate(lefts, axis=1), jnp.concatenate(rights, axis=1))
    width = 4 * owned
    total = sum(total[s * width : (s + 1) * width, :] for s in range(SPLITS)) + own_ref[...]
    for c in range(4):
        for b in range(owned):
            r = c * owned + b
            out_ref[c : c + 1, b * BLOCK : (b + 1) * BLOCK] = total[r : r + 1, :]


def shaped(*shape):
    return jax.ShapeDtypeStruct(shape, jnp.float32)


def per_device(
    sizes,
    old_state,
    send_blocks,
    node_slots,
    node_weights,
    front_mask,
    halo_lists,
    elem_nodes,
    shape_grads,
    elem_volume,
):
    old_state, send_blocks = old_state[0, 0, 0], send_blocks[0, 0, 0]
    slots = send_blocks.shape[1]
    send_blocks = send_blocks.reshape(-1, 1, slots)
    rows = FIELDS * slots
    arguments = [
        node_slots[0, 0, 0],
        node_weights[0, 0, 0],
        front_mask.reshape(-1, BLOCK),
        halo_lists.reshape(halo_lists.shape[-2], 1, -1),
        elem_nodes[0, 0, 0],
        shape_grads.reshape(-1, BLOCK),
        elem_volume[0, 0],
    ]
    old_rows = old_state.reshape(-1, BLOCK)
    count = len(arguments)
    cross, mine, *held = pl.pallas_call(
        functools.partial(pack_kernel, count),
        out_shape=[shaped(5, rows, BLOCK)] * 2 + [jax.ShapeDtypeStruct(a.shape, a.dtype) for a in arguments],
        in_specs=[pl.BlockSpec(memory_space=pltpu.HBM)] * (2 + count),
        out_specs=[VMEM] * (2 + count),
        scratch_shapes=[
            pltpu.SMEM(send_blocks.shape, jnp.int32),
            pltpu.VMEM(old_rows.shape, jnp.float32),
            pltpu.SemaphoreType.DMA((2 + count,)),
        ],
        compiler_params=params(),
    )(*(pltpu.with_memory_space_constraint(a, pltpu.HBM) for a in (send_blocks, old_rows, *arguments)))
    node_slots, node_weights, mask_rows, halos, elem_nodes, grad_rows, volume = held
    swap = lax.ppermute(cross, "layer", both_ways([(0, 1)]))
    moved = [
        lax.ppermute(jnp.stack([mine[q], swap[q]]), "mapx", pairs) for q, pairs in enumerate(column_moves(sizes[0]))
    ]

    owned = node_slots.shape[-1]
    slot_rows = node_slots.size // BLOCK
    found, node_rows, weight_rows, halo_rows = pl.pallas_call(
        near_kernel,
        out_shape=(
            shaped(FIELDS, slot_rows, BLOCK),
            jax.ShapeDtypeStruct((slot_rows, BLOCK), jnp.int32),
            shaped(slot_rows, BLOCK),
            jax.ShapeDtypeStruct((halos.size // BLOCK, BLOCK), jnp.int32),
        ),
        in_specs=[VMEM] * 6,
        out_specs=(VMEM,) * 4,
        compiler_params=params(),
    )(mine, swap, moved[0], node_slots, node_weights, halos)
    moves = 3 + sum(size > 2 for size in sizes)
    chunk = (2 * FIELDS, BLOCK)
    new_state, table, *ghosts = pl.pallas_call(
        functools.partial(state_kernel, sizes),
        out_shape=(shaped(FIELDS, owned), shaped(owned // (2 * BLOCK), *chunk)) + (shaped(*chunk),) * moves,
        in_specs=[VMEM] * 8,
        out_specs=(VMEM,) * (2 + moves),
        scratch_shapes=[pltpu.VMEM((6, *chunk), jnp.float32)],
        compiler_params=params(),
    )(*moved[1:], node_rows, found, weight_rows, mask_rows, halo_rows)
    ghosts = swap_all(ghosts, sizes)

    all_rows = elem_nodes.size // BLOCK
    slots_all = table.shape[0] + 6
    own, *sums = pl.pallas_call(
        functools.partial(element_kernel, sizes, moves),
        out_shape=(shaped(4 * owned // BLOCK, BLOCK),) + (shaped(8, BLOCK),) * moves,
        in_specs=[VMEM] * (4 + moves),
        out_specs=(VMEM,) * (1 + moves),
        scratch_shapes=[
            pltpu.VMEM((slots_all, *chunk), jnp.float32),
            pltpu.VMEM((all_rows, BLOCK), jnp.int32),
            pltpu.VMEM((all_rows // 4, BLOCK), jnp.float32),
            pltpu.VMEM((FIELDS, all_rows, BLOCK), jnp.float32),
            pltpu.VMEM((4 * SPLITS, all_rows, BLOCK), jnp.float32),
            pltpu.VMEM((6, 8, BLOCK), jnp.float32),
        ],
        compiler_params=params(),
    )(table, elem_nodes, grad_rows, volume, *ghosts)
    sums = swap_all(sums, sizes)
    residual = pl.pallas_call(
        functools.partial(residual_kernel, sizes, moves),
        out_shape=shaped(4, owned),
        in_specs=[VMEM] * (2 + moves),
        out_specs=VMEM,
        scratch_shapes=[pltpu.VMEM((6, 8, BLOCK), jnp.float32)],
        compiler_params=params(),
    )(own, halo_rows, *sums)
    return (new_state[None, None, None], residual[None, None, None])


def solution(mesh):
    sizes = tuple(mesh.shape[axis] for axis in AXES)
    row = P("mapx", "mapy", "layer", None)
    table = P("mapx", "mapy", "layer", None, None)
    return jax.shard_map(
        functools.partial(per_device, sizes),
        mesh=mesh,
        in_specs=(table, table, table, table, row, table, table, table, row),
        out_specs=(table, table),
        check_vma=False,
    )
```

profile of v0, /device:TPU:0, one launch (start us, length us, event | category | flops | bytes accessed | tf_op | source)
XLA Modules:
  0.0 41.8 jit_solution(18077751054176062910)
XLA Ops:
  0.6 1.5 %shard_map.104 = (f32[5,96,128]{2,1,0:T(8,128)S(1)}, f32[5,96,128]{2,1,0:T(8,128)S(1)}, s32[4,512]{1,0:T(4,128)S(1)}, f32[4,512]{1,0:T(4,128)S(1)}, s32[4,128]{1...) custom-call(s32[10,1,16]{2,1,0:T(1,128)} %bitcast.20, ...), custom_call_target="tpu_custom_call" | custom-call | tf_op jit(solution)/shard_map/pallas_call | solution.py:369
  2.2 0.5 %collective-permute-start = (f32[5,96,128]{2,1,0:T(8,128)S(1)}, f32[5,96,128]{2,1,0:T(8,128)S(1)}, u32[]{:S(2)}, u32[]{:S(2)}) collective-permute-start(f32[5,96,128]{2,1,0:T(8,128)S(1)} %get-tuple-element.27), channel_id=1, source_target_pairs={{0,1},{1,0},{2,3},{3,2},{4,5},{5,4},{6,7},{7,6},{8,9},{9,8},{10,11... | collective-permute-start | bytes 737288 | tf_op jit(solution)/shard_map/ppermute | solution.py:382
  2.7 1.1 %collective-permute-done.swap_ref = f32[5,96,128]{2,1,0:T(8,128)S(1)} collective-permute-done((f32[5,96,128]{2,1,0:T(8,128)S(1)}, f32[5,96,128]{2,1,0:T(8,128)S(1)}, u32[]{:S(2)}, u32[]{:S(2)}) %collective-permute-start) | collective-permute-done | bytes 245792 | tf_op jit(solution)/shard_map/ppermute | solution.py:382
  3.9 3.0 %collective-permute-start.1 = (f32[2,96,128]{2,1,0:T(8,128)S(1)}, f32[2,96,128]{2,1,0:T(8,128)S(1)}, u32[]{:S(2)}, u32[]{:S(2)}) collective-permute-start(f32[2,96,128]{2,1,0:T(8,128)S(1)} %pad_maximum_fusion), channel_id=1, source_target_pairs={{0,8},{8,0},{4,12},{12,4},{16,24},{24,16},{20,28},{28,20},{1,9},{9... | collective-permute-start | bytes 294920 | tf_op jit(solution)/shard_map/ppermute | solution.py:384
  6.9 0.7 %collective-permute-start.2 = (f32[2,96,128]{2,1,0:T(8,128)S(1)}, f32[2,96,128]{2,1,0:T(8,128)S(1)}, u32[]{:S(2)}, u32[]{:S(2)}) collective-permute-start(f32[2,96,128]{2,1,0:T(8,128)S(1)} %pad_maximum_fusion.1), channel_id=1, source_target_pairs={{8,16},{16,8},{12,20},{20,12},{9,17},{17,9},{13,21},{21,13},{10,18... | collective-permute-start | bytes 294920 | tf_op jit(solution)/shard_map/ppermute | solution.py:384
  7.6 0.7 %collective-permute-start.4 = (f32[2,96,128]{2,1,0:T(8,128)S(1)}, f32[2,96,128]{2,1,0:T(8,128)S(1)}, u32[]{:S(2)}, u32[]{:S(2)}) collective-permute-start(f32[2,96,128]{2,1,0:T(8,128)S(1)} %pad_maximum_fusion.3), channel_id=1, source_target_pairs={{4,8},{8,4},{12,16},{16,12},{20,24},{24,20},{5,9},{9,5},{13,17},{1... | collective-permute-start | bytes 294920 | tf_op jit(solution)/shard_map/ppermute | solution.py:384
  8.3 7.2 %collective-permute-start.3 = (f32[2,96,128]{2,1,0:T(8,128)S(1)}, f32[2,96,128]{2,1,0:T(8,128)S(1)}, u32[]{:S(2)}, u32[]{:S(2)}) collective-permute-start(f32[2,96,128]{2,1,0:T(8,128)S(1)} %pad_maximum_fusion.2), channel_id=1, source_target_pairs={{0,4},{4,0},{8,12},{12,8},{16,20},{20,16},{24,28},{28,24},{1,5},{5... | collective-permute-start | bytes 294920 | tf_op jit(solution)/shard_map/ppermute | solution.py:384
  15.4 0.0 collective-permute-done.4.next_ref
  15.4 0.9 %shard_map.105 = (f32[6,16,128]{2,1,0:T(8,128)S(1)}, s32[16,128]{1,0:T(8,128)S(1)}, f32[16,128]{1,0:T(8,128)S(1)}, s32[12,128]{1,0:T(8,128)S(1)}) custom-call(f32[5,96,128]{2,1,0:T(8,128)S(1)} %get-tuple-element.26.mine_ref, f32[5,96,128]{2,1,0:T(8,128)S(1)} %collective-permute-done.swap_ref, f32[2,96,128]{2,1,0:T(8,128)S(1)} %collective-permute-done.4.next_ref, ...), custom_call_target="tpu_custom_call" | custom-call | tf_op jit(solution)/shard_map/pallas_call | solution.py:389
  16.3 0.0 collective-permute-done.1.two_ref
  16.4 0.0 collective-permute-done.2.across_ref
  16.4 1.7 %collective-permute-done.3.pair_ref = f32[2,96,128]{2,1,0:T(8,128)S(1)} collective-permute-done((f32[2,96,128]{2,1,0:T(8,128)S(1)}, f32[2,96,128]{2,1,0:T(8,128)S(1)}, u32[]{:S(2)}, u32[]{:S(2)}) %collective-permute-start.3) | collective-permute-done | bytes 98336 | tf_op jit(solution)/shard_map/ppermute | solution.py:384
  18.0 1.4 %shard_map.106 = (f32[6,512]{1,0:T(8,128)S(1)}, f32[2,12,128]{2,1,0:T(8,128)S(1)}, f32[12,128]{1,0:T(8,128)S(1)}, f32[12,128]{1,0:T(8,128)S(1)}, f32[12,128]{1,0:T(8,128)S(1)}, /*index=5*/f32[12,128]{1,0:T(8,128)S(1)}) custom-call(f32[2,96,128]{2,1,0:T(8,128)S(1)} %collective-permute-done.1.two_ref, f32[2,96,128]{2,1,0:T(8,128)S(1)} %collective-permute-done.2.across_ref, ...), custom_call_target="tpu_custom_call" | custom-call | tf_op jit(solution)/shard_map/pallas_call | solution.py:403
  19.5 0.7 %collective-permute-start.5 = (f32[12,128]{1,0:T(8,128)S(1)}, f32[12,128]{1,0:T(8,128)S(1)}, u32[]{:S(2)}, u32[]{:S(2)}) collective-permute-start(f32[12,128]{1,0:T(8,128)S(1)} %get-tuple-element.41), channel_id=1, source_target_pairs={{4,8},{8,4},{12,16},{16,12},{20,24},{24,20},{5,9},{9,5},{13,17},{1... | collective-permute-start | bytes 18440 | tf_op jit(solution)/shard_map/ppermute | solution.py:49
  20.1 5.1 %collective-permute-start.6 = (f32[12,128]{1,0:T(8,128)S(1)}, f32[12,128]{1,0:T(8,128)S(1)}, u32[]{:S(2)}, u32[]{:S(2)}) collective-permute-start(f32[12,128]{1,0:T(8,128)S(1)} %get-tuple-element.42), channel_id=1, source_target_pairs={{0,4},{4,0},{8,12},{12,8},{16,20},{20,16},{24,28},{28,24},{1,5},{5... | collective-permute-start | bytes 18440 | tf_op jit(solution)/shard_map/ppermute | solution.py:49
  25.3 1.5 %collective-permute-start.7 = (f32[12,128]{1,0:T(8,128)S(1)}, f32[12,128]{1,0:T(8,128)S(1)}, u32[]{:S(2)}, u32[]{:S(2)}) collective-permute-start(f32[12,128]{1,0:T(8,128)S(1)} %get-tuple-element.43), channel_id=1, source_target_pairs={{0,2},{2,0},{1,3},{3,1},{4,6},{6,4},{5,7},{7,5},{8,10},{10,8},{9,1... | collective-permute-start | bytes 18440 | tf_op jit(solution)/shard_map/ppermute | solution.py:49
  26.8 0.0 collective-permute-start.8
  26.8 0.0 collective-permute-done.5.refs_4_
  26.8 0.1 collective-permute-done.6.refs_5_
  26.9 2.0 %collective-permute-done.7.refs_6_ = f32[12,128]{1,0:T(8,128)S(1)} collective-permute-done((f32[12,128]{1,0:T(8,128)S(1)}, f32[12,128]{1,0:T(8,128)S(1)}, u32[]{:S(2)}, u32[]{:S(2)}) %collective-permute-start.7) | collective-permute-done | bytes 6176 | tf_op jit(solution)/shard_map/ppermute | solution.py:49
  28.9 0.0 collective-permute-done.8.refs_7_
  28.9 3.7 %shard_map.107 = (f32[16,128]{1,0:T(8,128)S(1)}, f32[8,128]{1,0:T(8,128)S(1)}, f32[8,128]{1,0:T(8,128)S(1)}, f32[8,128]{1,0:T(8,128)S(1)}, f32[8,128]{1,0:T(8,128)S(1)}) custom-call(f32[2,12,128]{2,1,0:T(8,128)S(1)} %get-tuple-element.37.refs_0_, s32[4,2560]{1,0:T(4,128)S(1)} %get-tuple-element.38.refs_1_, f32[240,128]{1,0:T(8,128)S(1)} %get-tuple-element.39.refs_2_, ...), custom_call_target="tpu_custom_call" | custom-call | tf_op jit(solution)/shard_map/pallas_call | solution.py:415
  32.6 0.7 %collective-permute-start.9 = (f32[8,128]{1,0:T(8,128)S(1)}, f32[8,128]{1,0:T(8,128)S(1)}, u32[]{:S(2)}, u32[]{:S(2)}) collective-permute-start(f32[8,128]{1,0:T(8,128)S(1)} %get-tuple-element.46), channel_id=1, source_target_pairs={{4,8},{8,4},{12,16},{16,12},{20,24},{24,20},{5,9},{9,5},{13,17},{1... | collective-permute-start | bytes 12296 | tf_op jit(solution)/shard_map/ppermute | solution.py:49
  33.3 4.1 %collective-permute-start.10 = (f32[8,128]{1,0:T(8,128)S(1)}, f32[8,128]{1,0:T(8,128)S(1)}, u32[]{:S(2)}, u32[]{:S(2)}) collective-permute-start(f32[8,128]{1,0:T(8,128)S(1)} %get-tuple-element.47), channel_id=1, source_target_pairs={{0,4},{4,0},{8,12},{12,8},{16,20},{20,16},{24,28},{28,24},{1,5},{5... | collective-permute-start | bytes 12296 | tf_op jit(solution)/shard_map/ppermute | solution.py:49
  37.4 1.5 %collective-permute-start.11 = (f32[8,128]{1,0:T(8,128)S(1)}, f32[8,128]{1,0:T(8,128)S(1)}, u32[]{:S(2)}, u32[]{:S(2)}) collective-permute-start(f32[8,128]{1,0:T(8,128)S(1)} %get-tuple-element.48), channel_id=1, source_target_pairs={{0,2},{2,0},{1,3},{3,1},{4,6},{6,4},{5,7},{7,5},{8,10},{10,8},{9,1... | collective-permute-start | bytes 12296 | tf_op jit(solution)/shard_map/ppermute | solution.py:49
  38.9 0.0 collective-permute-start.12
  38.9 0.6 %copy.11 = f32[1,1,1,6,512]{4,2,3,1,0:T(1,128)} copy(f32[1,1,1,6,512]{4,3,2,1,0:T(8,128)S(1)} %bitcast.11) | data formatting | bytes 24576
  39.5 0.0 collective-permute-done.9.refs_2_
  39.5 0.0 collective-permute-done.10.refs_3_
  39.5 1.4 %collective-permute-done.11.refs_4_ = f32[8,128]{1,0:T(8,128)S(1)} collective-permute-done((f32[8,128]{1,0:T(8,128)S(1)}, f32[8,128]{1,0:T(8,128)S(1)}, u32[]{:S(2)}, u32[]{:S(2)}) %collective-permute-start.11) | collective-permute-done | bytes 4128 | tf_op jit(solution)/shard_map/ppermute | solution.py:49
  41.0 0.0 collective-permute-done.12.refs_5_
  41.0 0.9 %shard_map.108 = f32[4,512]{1,0:T(4,128)} custom-call(f32[16,128]{1,0:T(8,128)S(1)} %get-tuple-element.45.refs_0_, s32[12,128]{1,0:T(8,128)S(1)} %get-tuple-element.35.halos_ref.refs_1_, f32[8,128]{1,0:T(8,128)S(1)} %collective-permute-done.9.refs_2_, f32[8,128]{1,0:T(8,128)S(1)} %collective-permute-done.10.refs_3_, ...), custom_call_target="tpu_custom_call" | custom-call | tf_op jit(solution)/shard_map/pallas_call | solution.py:431
  (6 shorter events, 0.1 us)
Async XLA Ops:
  2.2 1.7 %collective-permute-start = (f32[5,96,128]{2,1,0:T(8,128)S(1)}, f32[5,96,128]{2,1,0:T(8,128)S(1)}, u32[]{:S(2)}, u32[]{:S(2)}) collective-permute-start(f32[5,96,128]{2,1,0:T(8,128)S(1)} %get-tuple-element.27), channel_id=1, source_target_pairs={{0,1},{1,0},{2,3},{3,2},{4,5},{5,4},{6,7},{7,6},{8,9},{9,8},{10,11... | collective-permute-start | bytes 737288 | tf_op jit(solution)/shard_map/ppermute | solution.py:382
  3.9 12.5 %collective-permute-start.1 = (f32[2,96,128]{2,1,0:T(8,128)S(1)}, f32[2,96,128]{2,1,0:T(8,128)S(1)}, u32[]{:S(2)}, u32[]{:S(2)}) collective-permute-start(f32[2,96,128]{2,1,0:T(8,128)S(1)} %pad_maximum_fusion), channel_id=1, source_target_pairs={{0,8},{8,0},{4,12},{12,4},{16,24},{24,16},{20,28},{28,20},{1,9},{9... | collective-permute-start | bytes 294920 | tf_op jit(solution)/shard_map/ppermute | solution.py:384
  6.9 9.5 %collective-permute-start.2 = (f32[2,96,128]{2,1,0:T(8,128)S(1)}, f32[2,96,128]{2,1,0:T(8,128)S(1)}, u32[]{:S(2)}, u32[]{:S(2)}) collective-permute-start(f32[2,96,128]{2,1,0:T(8,128)S(1)} %pad_maximum_fusion.1), channel_id=1, source_target_pairs={{8,16},{16,8},{12,20},{20,12},{9,17},{17,9},{13,21},{21,13},{10,18... | collective-permute-start | bytes 294920 | tf_op jit(solution)/shard_map/ppermute | solution.py:384
  7.6 7.9 %collective-permute-start.4 = (f32[2,96,128]{2,1,0:T(8,128)S(1)}, f32[2,96,128]{2,1,0:T(8,128)S(1)}, u32[]{:S(2)}, u32[]{:S(2)}) collective-permute-start(f32[2,96,128]{2,1,0:T(8,128)S(1)} %pad_maximum_fusion.3), channel_id=1, source_target_pairs={{4,8},{8,4},{12,16},{16,12},{20,24},{24,20},{5,9},{9,5},{13,17},{1... | collective-permute-start | bytes 294920 | tf_op jit(solution)/shard_map/ppermute | solution.py:384
  8.3 9.8 %collective-permute-start.3 = (f32[2,96,128]{2,1,0:T(8,128)S(1)}, f32[2,96,128]{2,1,0:T(8,128)S(1)}, u32[]{:S(2)}, u32[]{:S(2)}) collective-permute-start(f32[2,96,128]{2,1,0:T(8,128)S(1)} %pad_maximum_fusion.2), channel_id=1, source_target_pairs={{0,4},{4,0},{8,12},{12,8},{16,20},{20,16},{24,28},{28,24},{1,5},{5... | collective-permute-start | bytes 294920 | tf_op jit(solution)/shard_map/ppermute | solution.py:384
  19.5 7.3 %collective-permute-start.5 = (f32[12,128]{1,0:T(8,128)S(1)}, f32[12,128]{1,0:T(8,128)S(1)}, u32[]{:S(2)}, u32[]{:S(2)}) collective-permute-start(f32[12,128]{1,0:T(8,128)S(1)} %get-tuple-element.41), channel_id=1, source_target_pairs={{4,8},{8,4},{12,16},{16,12},{20,24},{24,20},{5,9},{9,5},{13,17},{1... | collective-permute-start | bytes 18440 | tf_op jit(solution)/shard_map/ppermute | solution.py:49
  20.1 6.8 %collective-permute-start.6 = (f32[12,128]{1,0:T(8,128)S(1)}, f32[12,128]{1,0:T(8,128)S(1)}, u32[]{:S(2)}, u32[]{:S(2)}) collective-permute-start(f32[12,128]{1,0:T(8,128)S(1)} %get-tuple-element.42), channel_id=1, source_target_pairs={{0,4},{4,0},{8,12},{12,8},{16,20},{20,16},{24,28},{28,24},{1,5},{5... | collective-permute-start | bytes 18440 | tf_op jit(solution)/shard_map/ppermute | solution.py:49
  25.3 3.7 %collective-permute-start.7 = (f32[12,128]{1,0:T(8,128)S(1)}, f32[12,128]{1,0:T(8,128)S(1)}, u32[]{:S(2)}, u32[]{:S(2)}) collective-permute-start(f32[12,128]{1,0:T(8,128)S(1)} %get-tuple-element.43), channel_id=1, source_target_pairs={{0,2},{2,0},{1,3},{3,1},{4,6},{6,4},{5,7},{7,5},{8,10},{10,8},{9,1... | collective-permute-start | bytes 18440 | tf_op jit(solution)/shard_map/ppermute | solution.py:49
  26.8 2.1 %collective-permute-start.8 = (f32[12,128]{1,0:T(8,128)S(1)}, f32[12,128]{1,0:T(8,128)S(1)}, u32[]{:S(2)}, u32[]{:S(2)}) collective-permute-start(f32[12,128]{1,0:T(8,128)S(1)} %get-tuple-element.44), channel_id=1, source_target_pairs={{0,1},{1,0},{2,3},{3,2},{4,5},{5,4},{6,7},{7,6},{8,9},{9,8},{10,11... | collective-permute-start | bytes 18440 | tf_op jit(solution)/shard_map/ppermute | solution.py:49
  32.6 6.9 %collective-permute-start.9 = (f32[8,128]{1,0:T(8,128)S(1)}, f32[8,128]{1,0:T(8,128)S(1)}, u32[]{:S(2)}, u32[]{:S(2)}) collective-permute-start(f32[8,128]{1,0:T(8,128)S(1)} %get-tuple-element.46), channel_id=1, source_target_pairs={{4,8},{8,4},{12,16},{16,12},{20,24},{24,20},{5,9},{9,5},{13,17},{1... | collective-permute-start | bytes 12296 | tf_op jit(solution)/shard_map/ppermute | solution.py:49
  33.3 6.2 %collective-permute-start.10 = (f32[8,128]{1,0:T(8,128)S(1)}, f32[8,128]{1,0:T(8,128)S(1)}, u32[]{:S(2)}, u32[]{:S(2)}) collective-permute-start(f32[8,128]{1,0:T(8,128)S(1)} %get-tuple-element.47), channel_id=1, source_target_pairs={{0,4},{4,0},{8,12},{12,8},{16,20},{20,16},{24,28},{28,24},{1,5},{5... | collective-permute-start | bytes 12296 | tf_op jit(solution)/shard_map/ppermute | solution.py:49
  37.4 3.6 %collective-permute-start.11 = (f32[8,128]{1,0:T(8,128)S(1)}, f32[8,128]{1,0:T(8,128)S(1)}, u32[]{:S(2)}, u32[]{:S(2)}) collective-permute-start(f32[8,128]{1,0:T(8,128)S(1)} %get-tuple-element.48), channel_id=1, source_target_pairs={{0,2},{2,0},{1,3},{3,1},{4,6},{6,4},{5,7},{7,5},{8,10},{10,8},{9,1... | collective-permute-start | bytes 12296 | tf_op jit(solution)/shard_map/ppermute | solution.py:49
  38.9 2.1 %collective-permute-start.12 = (f32[8,128]{1,0:T(8,128)S(1)}, f32[8,128]{1,0:T(8,128)S(1)}, u32[]{:S(2)}, u32[]{:S(2)}) collective-permute-start(f32[8,128]{1,0:T(8,128)S(1)} %get-tuple-element.49), channel_id=1, source_target_pairs={{0,1},{1,0},{2,3},{3,2},{4,5},{5,4},{6,7},{7,6},{8,9},{9,8},{10,11... | collective-permute-start | bytes 12296 | tf_op jit(solution)/shard_map/ppermute | solution.py:49
where the time goes:
time: 42.1 us; the launch traced here: 41.8 us
  starting transfers between devices  25.6 us (61%)
  Pallas kernels  8.46 us (20%)
  waiting for transfers between devices  6.37 us (15%)
  between operations  0.74 us (2%)
  local copies, waits for them, and re-layouts  0.64 us (2%)
    ppermute x8, starting transfers between devices, pair_swap(): lax.ppermute(value, axis, both_ways([(at, at + 1) for at in range(first,...  13.6 us
    ppermute x4, starting transfers between devices, per_device(): lax.ppermute(jnp.stack([mine[q], swap[q]]), 'mapx', pairs)  11.5 us
    pallas_call x1, Pallas kernels, per_device(): pl.pallas_call(functools.partial(element_kernel, sizes, moves), out_shape...  3.69 us
    ppermute x8, waiting for transfers between devices, pair_swap(): lax.ppermute(value, axis, both_ways([(at, at + 1) for at in range(first,...  3.58 us
    ppermute x4, waiting for transfers between devices, per_device(): lax.ppermute(jnp.stack([mine[q], swap[q]]), 'mapx', pairs)  1.66 us
    pallas_call x1, Pallas kernels, per_device(): pl.pallas_call(functools.partial(pack_kernel, count), out_shape=[shaped(5...  1.53 us
    pallas_call x1, Pallas kernels, per_device(): pl.pallas_call(functools.partial(state_kernel, sizes), out_shape=(shaped(...  1.44 us
    ppermute x1, waiting for transfers between devices, per_device(): swap = lax.ppermute(cross, 'layer', both_ways([(0, 1)]))  1.12 us
  transfers between devices with their start and end apart: 13, of which 5 were waited for; matrix products, arithmetic and copies ran while one was open for 2% of the time, Pallas kernels for 2%

commit v1 on v0

--- a/solution.py
+++ b/solution.py
@@ -57,12 +57,12 @@
 
 def pack_kernel(count, *refs):
     blocks_in_ref, old_in_ref = refs[:2]
-    cross_ref, mine_ref = refs[2 + count : 4 + count]
-    blocks_ref, old_ref, sems = refs[4 + 2 * count :]
+    cross_first_ref, cross_ref, mine_first_ref, mine_ref = refs[2 + count : 6 + count]
+    blocks_ref, old_ref, sems = refs[6 + 2 * count :]
     first = [pltpu.make_async_copy(blocks_in_ref, blocks_ref, sems.at[0])]
     first += [pltpu.make_async_copy(old_in_ref, old_ref, sems.at[1])]
     rest = [
-        pltpu.make_async_copy(refs[2 + i], refs[4 + count + i], sems.at[2 + i]) for i in range(count)
+        pltpu.make_async_copy(refs[2 + i], refs[6 + count + i], sems.at[2 + i]) for i in range(count)
     ]
     for copy in first + rest:
         copy.start()
@@ -72,12 +72,13 @@
     stride = old_ref.shape[0] // FIELDS
     layer = lax.axis_index("layer")
     offsets = column_offsets()
-    for out_ref, to_layer in ((cross_ref, 1 - layer), (mine_ref, layer)):
+    for first_ref, out_ref, to_layer in ((cross_first_ref, cross_ref, 1 - layer), (mine_first_ref, mine_ref, layer)):
         for q, offset in enumerate(offsets):
             peer = (offset + REACH) * 2 + to_layer
+            chunk_ref = first_ref.at[0] if q == 0 else out_ref.at[q - 1]
             for c in range(slots):
                 rows = pl.ds(blocks_ref[peer, 0, c], FIELDS, stride=stride)
-                out_ref[q, FIELDS * c : FIELDS * (c + 1), :] = old_ref[rows, :]
+                chunk_ref[FIELDS * c : FIELDS * (c + 1), :] = old_ref[rows, :]
     for copy in rest:
         copy.wait()
 
@@ -119,27 +120,61 @@
             to_ref[r * count + i : r * count + i + 1, :] = from_ref[r : r + 1, i * BLOCK : (i + 1) * BLOCK]
 
 
+def lane_one_hot(ids):
+    lanes = (ids & (BLOCK - 1)).astype(jnp.float32).astype(jnp.bfloat16)
+    rows = lax.broadcasted_iota(jnp.int32, (BLOCK, BLOCK), 0).astype(jnp.float32).astype(jnp.bfloat16)
+    hit = rows == jnp.broadcast_to(lanes, rows.shape)
+    return jnp.where(hit, jnp.ones_like(rows), jnp.zeros_like(rows))
+
+
 def near_kernel(
-    mine_ref, swap_ref, next_ref, slots_in_ref, weights_in_ref, halos_in_ref, found_ref, slots_ref, weights_ref, halos_ref
+    mine_ref,
+    swap_ref,
+    slots_in_ref,
+    weights_in_ref,
+    halos_in_ref,
+    nodes_in_ref,
+    volume_in_ref,
+    found_ref,
+    slots_ref,
+    weights_ref,
+    halos_ref,
+    nodes_ref,
+    volume_ref,
+    halo_hot_ref,
+    node_hot_ref,
 ):
     for k in range(halos_in_ref.shape[0]):
         cut_rows(halos_in_ref.at[k], halos_ref.at[2 * k : 2 * k + 2])
     cut_rows(slots_in_ref, slots_ref)
     cut_rows(weights_in_ref, weights_ref)
+    cut_rows(nodes_in_ref, nodes_ref)
+    cut_rows(volume_in_ref, volume_ref)
     slots = mine_ref.shape[1] // FIELDS
-    offsets = column_offsets()
     for v in range(slots_ref.shape[0] // 8):
         ids = slots_ref[8 * v : 8 * v + 8, :]
         blocks, lanes = ids >> 7, ids & (BLOCK - 1)
         found = tuple(jnp.zeros((8, BLOCK), jnp.float32) for _ in range(FIELDS))
-        for ref, chunk, q, other in ((mine_ref, 4, 4, 0), (swap_ref, 4, 4, 1), (next_ref, 0, 0, 0), (next_ref, 1, 0, 1)):
-            found = add_blocks(ref, chunk, first_block(offsets[q], other, slots), blocks, lanes, found)
+        for ref, other in ((mine_ref, 0), (swap_ref, 1)):
+            found = add_blocks(ref, 3, first_block(0, other, slots), blocks, lanes, found)
         for f in range(FIELDS):
             found_ref[f, 8 * v : 8 * v + 8, :] = found[f]
+    for r in range(halos_ref.shape[0]):
+        halo_hot_ref[:, r * BLOCK : (r + 1) * BLOCK] = lane_one_hot(halos_ref[r : r + 1, :])
+    steps, _, width = node_hot_ref.shape
+    group = width // BLOCK
+
+    def hot(step, carry):
+        for r in range(group):
+            ids = nodes_ref[pl.ds(step * group + r, 1), :]
+            node_hot_ref[step, :, r * BLOCK : (r + 1) * BLOCK] = lane_one_hot(ids)
+        return carry
+
+    lax.fori_loop(0, steps, hot, 0)
 
 
 def state_kernel(
-    counts, two_ref, across_ref, pair_ref, slots_ref, found_ref, weights_ref, mask_ref, halos_ref, state_ref, table_ref, *more_refs
+    counts, next_ref, two_ref, across_ref, pair_ref, slots_ref, found_ref, weights_ref, mask_ref, halos_ref, state_ref, table_ref, *more_refs
 ):
     send_refs, cut_ref = more_refs[:-1], more_refs[-1]
     slots = two_ref.shape[1] // FIELDS
@@ -150,7 +185,7 @@
         ids = slots_ref[8 * v : 8 * v + 8, :]
         blocks, lanes = ids >> 7, ids & (BLOCK - 1)
         fields = tuple(found_ref[f, 8 * v : 8 * v + 8, :] for f in range(FIELDS))
-        for q, ref in ((1, two_ref), (2, across_ref), (3, pair_ref)):
+        for q, ref in enumerate((next_ref, two_ref, across_ref, pair_ref)):
             for other in range(2):
                 fields = add_blocks(ref, other, first_block(offsets[q], other, slots), blocks, lanes, fields)
         found.append(fields)
@@ -164,8 +199,7 @@
                 total = total + term[k * rows : (k + 1) * rows, :]
         if f == 4:
             total = jnp.where(front, ocean_temp, total)
-        for r in range(rows):
-            state_ref[f : f + 1, r * BLOCK : (r + 1) * BLOCK] = total[r : r + 1, :]
+        state_ref[f * rows : (f + 1) * rows, :] = total
         for s in range(rows // 2):
             table_ref[s, 2 * f : 2 * f + 2, :] = total[2 * s : 2 * s + 2, :]
     starts = (0, halos_ref.shape[0] - 8)
@@ -211,14 +245,11 @@
     return result
 
 
-def one_hot_sum(values, ids, block_count):
+def placed(values, ids, block_count):
     rows = lax.broadcasted_iota(jnp.int32, (block_count, BLOCK), 0)
     hit = rows == jnp.broadcast_to(ids >> 7, rows.shape)
     left = [jnp.where(hit, jnp.broadcast_to(v, rows.shape), 0.0) for v in values]
-    left = jnp.concatenate(left, axis=0).astype(jnp.bfloat16)
-    lanes = lax.broadcasted_iota(jnp.int32, (BLOCK, BLOCK), 0)
-    right = jnp.where(lanes == jnp.broadcast_to(ids & (BLOCK - 1), lanes.shape), 1.0, 0.0).astype(jnp.bfloat16)
-    return left, right
+    return jnp.concatenate(left, axis=0).astype(jnp.bfloat16)
 
 
 def cut_parts(value):
@@ -235,18 +266,16 @@
 
 
 def element_kernel(counts, moves, *refs):
-    table_in_ref, nodes_in_ref, grads_ref, volume_in_ref = refs[:4]
-    came_refs = refs[4 : 4 + moves]
-    own_ref = refs[4 + moves]
-    send_refs = refs[5 + moves : 5 + 2 * moves]
-    table_ref, nodes_ref, volume_ref, values_ref, parts_ref, cut_ref = refs[5 + 2 * moves :]
+    table_in_ref, nodes_ref, node_hot_ref, grads_ref, volume_ref = refs[:5]
+    came_refs = refs[5 : 5 + moves]
+    own_ref = refs[5 + moves]
+    send_refs = refs[6 + moves : 6 + 2 * moves]
+    table_ref, values_ref, parts_ref, cut_ref = refs[6 + 2 * moves :]
     owned_slots = table_in_ref.shape[0]
     table_ref[0:owned_slots] = table_in_ref[...]
     for axis, (place_at, inside, outside) in enumerate(arrivals(counts, came_refs)):
         table_ref[owned_slots + 2 * axis + 1 - place_at] = inside
         table_ref[owned_slots + 2 * axis + place_at] = outside
-    cut_rows(nodes_in_ref, nodes_ref)
-    cut_rows(volume_in_ref, volume_ref)
     block_count = 2 * table_ref.shape[0]
     all_rows = nodes_ref.shape[0]
     elem_rows = all_rows // 4
@@ -286,17 +315,15 @@
                 for s, part in enumerate(cut_parts(force)):
                     parts_ref[i * SPLITS + s, at[a], :] = part
 
-    group = 10
+    group = node_hot_ref.shape[2] // BLOCK
 
     def gather_terms(step, total):
-        lefts, rights = [], []
+        lefts = []
         for r in range(group):
             at = pl.ds(step * group + r, 1)
             terms = [parts_ref[c * SPLITS + s, at, :] for s in range(SPLITS) for c in range(4)]
-            left, right = one_hot_sum(terms, nodes_ref[at, :], block_count)
-            lefts.append(left)
-            rights.append(right)
-        return total + nt_dot(jnp.concatenate(lefts, axis=1), jnp.concatenate(rights, axis=1))
+            lefts.append(placed(terms, nodes_ref[at, :], block_count))
+        return total + nt_dot(jnp.concatenate(lefts, axis=1), node_hot_ref[step])
 
     width = 4 * block_count
     total = lax.fori_loop(0, all_rows // group, gather_terms, jnp.zeros((SPLITS * width, BLOCK), jnp.float32))
@@ -311,22 +338,20 @@
 
 
 def residual_kernel(counts, moves, *refs):
-    own_ref, halos_ref = refs[:2]
-    out_ref, came_ref = refs[2 + moves :]
-    for axis, (place_at, inside, outside) in enumerate(arrivals(counts, refs[2 : 2 + moves])):
+    own_ref, halos_ref, halo_hot_ref = refs[:3]
+    out_ref, came_ref = refs[3 + moves :]
+    for axis, (place_at, inside, outside) in enumerate(arrivals(counts, refs[3 : 3 + moves])):
         came_ref[2 * axis + place_at] = inside
         came_ref[2 * axis + 1 - place_at] = outside
     owned = own_ref.shape[0] // 4
-    lefts, rights = [], []
+    lefts = []
     for k in range(6):
         parts = cut_parts(came_ref[k])
         for h in range(2):
             ids = halos_ref[2 * k + h : 2 * k + h + 1, :]
             terms = [parts[s][2 * c + h : 2 * c + h + 1, :] for s in range(SPLITS) for c in range(4)]
-            left, right = one_hot_sum(terms, ids, owned)
-            lefts.append(left)
-            rights.append(right)
-    total = nt_dot(jnp.concatenate(lefts, axis=1), jnp.concatenate(rights, axis=1))
+            lefts.append(placed(terms, ids, owned))
+    total = nt_dot(jnp.concatenate(lefts, axis=1), halo_hot_ref[...])
     width = 4 * owned
     total = sum(total[s * width : (s + 1) * width, :] for s in range(SPLITS)) + own_ref[...]
     for c in range(4):
@@ -366,11 +391,11 @@
     ]
     old_rows = old_state.reshape(-1, BLOCK)
     count = len(arguments)
-    cross, mine, *held = pl.pallas_call(
+    cross_first, cross, mine_first, mine, *held = pl.pallas_call(
         functools.partial(pack_kernel, count),
-        out_shape=[shaped(5, rows, BLOCK)] * 2 + [jax.ShapeDtypeStruct(a.shape, a.dtype) for a in arguments],
+        out_shape=[shaped(1, rows, BLOCK), shaped(4, rows, BLOCK)] * 2 + [jax.ShapeDtypeStruct(a.shape, a.dtype) for a in arguments],
         in_specs=[pl.BlockSpec(memory_space=pltpu.HBM)] * (2 + count),
-        out_specs=[VMEM] * (2 + count),
+        out_specs=[VMEM] * (4 + count),
         scratch_shapes=[
             pltpu.SMEM(send_blocks.shape, jnp.int32),
             pltpu.VMEM(old_rows.shape, jnp.float32),
@@ -379,64 +404,70 @@
         compiler_params=params(),
     )(*(pltpu.with_memory_space_constraint(a, pltpu.HBM) for a in (send_blocks, old_rows, *arguments)))
     node_slots, node_weights, mask_rows, halos, elem_nodes, grad_rows, volume = held
-    swap = lax.ppermute(cross, "layer", both_ways([(0, 1)]))
-    moved = [
-        lax.ppermute(jnp.stack([mine[q], swap[q]]), "mapx", pairs) for q, pairs in enumerate(column_moves(sizes[0]))
-    ]
+    layers = both_ways([(0, 1)])
+    swap_first = lax.ppermute(cross_first, "layer", layers)
+    swap = lax.ppermute(cross, "layer", layers)
+    both = [jnp.concatenate([mine_first, swap_first])] + [jnp.stack([mine[q], swap[q]]) for q in range(3)]
+    moved = [lax.ppermute(pair, "mapx", pairs) for pair, pairs in zip(both, column_moves(sizes[0]))]
 
     owned = node_slots.shape[-1]
     slot_rows = node_slots.size // BLOCK
-    found, node_rows, weight_rows, halo_rows = pl.pallas_call(
+    all_rows = elem_nodes.size // BLOCK
+    halo_count = halos.size // BLOCK
+    hot_steps = next(n for n in (8, 4, 2, 1) if all_rows % n == 0)
+    whole = lambda *shape: jax.ShapeDtypeStruct(shape, jnp.int32)
+    found, slots_cut, weights_cut, halos_cut, nodes_cut, volume_cut, halo_hot, node_hot = pl.pallas_call(
         near_kernel,
         out_shape=(
             shaped(FIELDS, slot_rows, BLOCK),
-            jax.ShapeDtypeStruct((slot_rows, BLOCK), jnp.int32),
+            whole(slot_rows, BLOCK),
             shaped(slot_rows, BLOCK),
-            jax.ShapeDtypeStruct((halos.size // BLOCK, BLOCK), jnp.int32),
+            whole(halo_count, BLOCK),
+            whole(all_rows, BLOCK),
+            shaped(all_rows // 4, BLOCK),
+            jax.ShapeDtypeStruct((BLOCK, halo_count * BLOCK), jnp.bfloat16),
+            jax.ShapeDtypeStruct((hot_steps, BLOCK, all_rows // hot_steps * BLOCK), jnp.bfloat16),
         ),
-        in_specs=[VMEM] * 6,
-        out_specs=(VMEM,) * 4,
+        in_specs=[VMEM] * 7,
+        out_specs=(VMEM,) * 8,
         compiler_params=params(),
-    )(mine, swap, moved[0], node_slots, node_weights, halos)
+    )(mine, swap, node_slots, node_weights, halos, elem_nodes, volume)
     moves = 3 + sum(size > 2 for size in sizes)
     chunk = (2 * FIELDS, BLOCK)
     new_state, table, *ghosts = pl.pallas_call(
         functools.partial(state_kernel, sizes),
-        out_shape=(shaped(FIELDS, owned), shaped(owned // (2 * BLOCK), *chunk)) + (shaped(*chunk),) * moves,
-        in_specs=[VMEM] * 8,
+        out_shape=(shaped(FIELDS * owned // BLOCK, BLOCK), shaped(owned // (2 * BLOCK), *chunk)) + (shaped(*chunk),) * moves,
+        in_specs=[VMEM] * 9,
         out_specs=(VMEM,) * (2 + moves),
         scratch_shapes=[pltpu.VMEM((6, *chunk), jnp.float32)],
         compiler_params=params(),
-    )(*moved[1:], node_rows, found, weight_rows, mask_rows, halo_rows)
+    )(*moved, slots_cut, found, weights_cut, mask_rows, halos_cut)
     ghosts = swap_all(ghosts, sizes)
 
-    all_rows = elem_nodes.size // BLOCK
     slots_all = table.shape[0] + 6
     own, *sums = pl.pallas_call(
         functools.partial(element_kernel, sizes, moves),
         out_shape=(shaped(4 * owned // BLOCK, BLOCK),) + (shaped(8, BLOCK),) * moves,
-        in_specs=[VMEM] * (4 + moves),
+        in_specs=[VMEM] * (5 + moves),
         out_specs=(VMEM,) * (1 + moves),
         scratch_shapes=[
             pltpu.VMEM((slots_all, *chunk), jnp.float32),
-            pltpu.VMEM((all_rows, BLOCK), jnp.int32),
-            pltpu.VMEM((all_rows // 4, BLOCK), jnp.float32),
             pltpu.VMEM((FIELDS, all_rows, BLOCK), jnp.float32),
             pltpu.VMEM((4 * SPLITS, all_rows, BLOCK), jnp.float32),
             pltpu.VMEM((6, 8, BLOCK), jnp.float32),
         ],
         compiler_params=params(),
-    )(table, elem_nodes, grad_rows, volume, *ghosts)
+    )(table, nodes_cut, node_hot, grad_rows, volume_cut, *ghosts)
     sums = swap_all(sums, sizes)
     residual = pl.pallas_call(
         functools.partial(residual_kernel, sizes, moves),
         out_shape=shaped(4, owned),
-        in_specs=[VMEM] * (2 + moves),
+        in_specs=[VMEM] * (3 + moves),
         out_specs=VMEM,
         scratch_shapes=[pltpu.VMEM((6, 8, BLOCK), jnp.float32)],
         compiler_params=params(),
-    )(own, halo_rows, *sums)
-    return (new_state[None, None, None], residual[None, None, None])
+    )(own, halos_cut, halo_hot, *sums)
+    return (new_state.reshape(1, 1, 1, FIELDS, owned), residual[None, None, None])
 
 
 def solution(mesh):

time: 42.1 us -> 41.7 us (level)
  starting transfers between devices: 25.6 us -> 24.4 us
  Pallas kernels: 8.46 us -> 9.26 us
  local copies, waits for them, and re-layouts: 0.64 us -> 0.02 us
  waiting for transfers between devices: 6.37 us -> 6.95 us
    ppermute x8, starting transfers between devices: 13.6 us -> 12.4 us  [pair_swap(): lax.ppermute(value, axis, both_ways([(at, at + 1) for at in range(first,...]
    pallas_call x1, Pallas kernels: 1.44 us -> 2.35 us  [per_device(): pl.pallas_call(functools.partial(state_kernel, sizes), out_shape=(shaped(...]
    ppermute x8, waiting for transfers between devices: 3.58 us -> 4.22 us  [pair_swap(): lax.ppermute(value, axis, both_ways([(at, at + 1) for at in range(first,...]
    unnamed x1 -> x0, local copies, waits for them, and re-layouts: 0.61 us -> none
    ppermute x5 -> x6, waiting for transfers between devices: 2.78 us -> 2.74 us  [the longest x4 1.6 us: per_device(): lax.ppermute(pair, 'mapx', pairs)]
    ppermute x5 -> x6, starting transfers between devices: 12 us -> 12 us  [the longest x4 11.4 us: per_device(): lax.ppermute(pair, 'mapx', pairs)]
  transfers between devices with their start and end apart: 13 -> 14, of which waited for: 5 -> 6; matrix products, arithmetic and copies ran while one was open for 2% -> 0% of each run, Pallas kernels for 2% -> 2%
where the time goes in v1:
time: 41.7 us; the launch traced here: 41.4 us
  starting transfers between devices  24.4 us (59%)
  Pallas kernels  9.26 us (22%)
  waiting for transfers between devices  6.95 us (17%)
  between operations  0.75 us (2%)
    ppermute x8, starting transfers between devices, pair_swap(): lax.ppermute(value, axis, both_ways([(at, at + 1) for at in range(first,...  12.4 us
    ppermute x4, starting transfers between devices, per_device(): lax.ppermute(pair, 'mapx', pairs)  11.4 us
    ppermute x8, waiting for transfers between devices, pair_swap(): lax.ppermute(value, axis, both_ways([(at, at + 1) for at in range(first,...  4.22 us
    pallas_call x1, Pallas kernels, per_device(): pl.pallas_call(functools.partial(element_kernel, sizes, moves), out_shape...  3.56 us
    pallas_call x1, Pallas kernels, per_device(): pl.pallas_call(functools.partial(state_kernel, sizes), out_shape=(shaped(...  2.35 us
    ppermute x4, waiting for transfers between devices, per_device(): lax.ppermute(pair, 'mapx', pairs)  1.6 us
    pallas_call x1, Pallas kernels, per_device(): pl.pallas_call(functools.partial(pack_kernel, count), out_shape=[shaped(1...  1.53 us
    ppermute x1, waiting for transfers between devices, per_device(): swap_first = lax.ppermute(cross_first, 'layer', layers)  1.14 us
  transfers between devices with their start and end apart: 14, of which 6 were waited for; matrix products, arithmetic and copies ran while one was open for 0% of the time, Pallas kernels for 2%

profile of v1, /device:TPU:0, one launch (start us, length us, event | category | flops | bytes accessed | tf_op | source)
XLA Modules:
  0.0 41.4 jit_solution(449904523875430872)
XLA Ops:
  0.6 1.5 %shard_map.104 = (f32[1,96,128]{2,1,0:T(8,128)S(1)}, f32[4,96,128]{2,1,0:T(8,128)S(1)}, f32[1,96,128]{2,1,0:T(8,128)S(1)}, f32[4,96,128]{2,1,0:T(8,128)S(1)}, s3...) custom-call(s32[10,1,16]{2,1,0:T(1,128)} %bitcast.19, ...), custom_call_target="tpu_custom_call" | custom-call | tf_op jit(solution)/shard_map/pallas_call | solution.py:394
  2.2 0.5 %collective-permute-start.2 = (f32[4,96,128]{2,1,0:T(8,128)S(1)}, f32[4,96,128]{2,1,0:T(8,128)S(1)}, u32[]{:S(2)}, u32[]{:S(2)}) collective-permute-start(f32[4,96,128]{2,1,0:T(8,128)S(1)} %get-tuple-element.35), channel_id=1, source_target_pairs={{0,1},{1,0},{2,3},{3,2},{4,5},{5,4},{6,7},{7,6},{8,9},{9,8},{10,11... | collective-permute-start | bytes 589832 | tf_op jit(solution)/shard_map/ppermute | solution.py:409
  2.7 0.1 collective-permute-start
  2.8 1.1 %collective-permute-done = f32[1,96,128]{2,1,0:T(8,128)S(1)} collective-permute-done((f32[1,96,128]{2,1,0:T(8,128)S(1)}, f32[1,96,128]{2,1,0:T(8,128)S(1)}, u32[]{:S(2)}, u32[]{:S(2)}) %collective-permute-start) | collective-permute-done | bytes 49184 | tf_op jit(solution)/shard_map/ppermute | solution.py:408
  3.9 0.7 %collective-permute-start.1 = (f32[2,96,128]{2,1,0:T(8,128)S(1)}, f32[2,96,128]{2,1,0:T(8,128)S(1)}, u32[]{:S(2)}, u32[]{:S(2)}) collective-permute-start(f32[2,96,128]{2,1,0:T(8,128)S(1)} %pad_maximum_fusion), channel_id=1, source_target_pairs={{4,8},{8,4},{12,16},{16,12},{20,24},{24,20},{5,9},{9,5},{13,17},{1... | collective-permute-start | bytes 294920 | tf_op jit(solution)/shard_map/ppermute | solution.py:411
  4.6 0.0 collective-permute-done.2.swap_ref
  4.7 5.6 %collective-permute-start.5 = (f32[2,96,128]{2,1,0:T(8,128)S(1)}, f32[2,96,128]{2,1,0:T(8,128)S(1)}, u32[]{:S(2)}, u32[]{:S(2)}) collective-permute-start(f32[2,96,128]{2,1,0:T(8,128)S(1)} %pad_maximum_fusion.3), channel_id=1, source_target_pairs={{0,4},{4,0},{8,12},{12,8},{16,20},{20,16},{24,28},{28,24},{1,5},{5... | collective-permute-start | bytes 294920 | tf_op jit(solution)/shard_map/ppermute | solution.py:411
  10.3 0.7 %collective-permute-start.4 = (f32[2,96,128]{2,1,0:T(8,128)S(1)}, f32[2,96,128]{2,1,0:T(8,128)S(1)}, u32[]{:S(2)}, u32[]{:S(2)}) collective-permute-start(f32[2,96,128]{2,1,0:T(8,128)S(1)} %pad_maximum_fusion.2), channel_id=1, source_target_pairs={{8,16},{16,8},{12,20},{20,12},{9,17},{17,9},{13,21},{21,13},{10,18... | collective-permute-start | bytes 294920 | tf_op jit(solution)/shard_map/ppermute | solution.py:411
  11.0 4.5 %collective-permute-start.3 = (f32[2,96,128]{2,1,0:T(8,128)S(1)}, f32[2,96,128]{2,1,0:T(8,128)S(1)}, u32[]{:S(2)}, u32[]{:S(2)}) collective-permute-start(f32[2,96,128]{2,1,0:T(8,128)S(1)} %pad_maximum_fusion.1), channel_id=1, source_target_pairs={{0,8},{8,0},{4,12},{12,4},{16,24},{24,16},{20,28},{28,20},{1,9},{9... | collective-permute-start | bytes 294920 | tf_op jit(solution)/shard_map/ppermute | solution.py:411
  15.4 1.0 %shard_map.105 = (f32[6,16,128]{2,1,0:T(8,128)S(1)}, s32[16,128]{1,0:T(8,128)S(1)}, f32[16,128]{1,0:T(8,128)S(1)}, s32[12,128]{1,0:T(8,128)S(1)}, s32[80,128]{1,...) custom-call(f32[4,96,128]{2,1,0:T(8,128)S(1)} %get-tuple-element.34.mine_ref, ...), custom_call_target="tpu_custom_call" | custom-call | tf_op jit(solution)/shard_map/pallas_call | solution.py:419
  16.4 0.0 collective-permute-done.1.next_ref
  16.4 0.0 collective-permute-done.5.pair_ref
  16.4 0.0 collective-permute-done.4.across_ref
  16.4 1.6 %collective-permute-done.3.two_ref = f32[2,96,128]{2,1,0:T(8,128)S(1)} collective-permute-done((f32[2,96,128]{2,1,0:T(8,128)S(1)}, f32[2,96,128]{2,1,0:T(8,128)S(1)}, u32[]{:S(2)}, u32[]{:S(2)}) %collective-permute-start.3) | collective-permute-done | bytes 98336 | tf_op jit(solution)/shard_map/ppermute | solution.py:411
  18.0 2.3 %shard_map.106 = (f32[24,128]{1,0:T(8,128)}, f32[2,12,128]{2,1,0:T(8,128)S(1)}, f32[12,128]{1,0:T(8,128)S(1)}, f32[12,128]{1,0:T(8,128)S(1)}, f32[12,128]{1,0:T(8,128)S(1)}, /*index=5*/f32[12,128]{1,0:T(8,128)S(1)}) custom-call(f32[2,96,128]{2,1,0:T(8,128)S(1)} %collective-permute-done.1.next_ref, f32[2,96,128]{2,1,0:T(8,128)S(1)} %collective-permute-done.3.two_ref, ...), custom_call_target="tpu_custom_call" | custom-call | tf_op jit(solution)/shard_map/pallas_call | solution.py:437
  20.4 0.6 %collective-permute-start.6 = (f32[12,128]{1,0:T(8,128)S(1)}, f32[12,128]{1,0:T(8,128)S(1)}, u32[]{:S(2)}, u32[]{:S(2)}) collective-permute-start(f32[12,128]{1,0:T(8,128)S(1)} %get-tuple-element.52), channel_id=1, source_target_pairs={{4,8},{8,4},{12,16},{16,12},{20,24},{24,20},{5,9},{9,5},{13,17},{1... | collective-permute-start | bytes 18440 | tf_op jit(solution)/shard_map/ppermute | solution.py:49
  21.0 4.8 %collective-permute-start.7 = (f32[12,128]{1,0:T(8,128)S(1)}, f32[12,128]{1,0:T(8,128)S(1)}, u32[]{:S(2)}, u32[]{:S(2)}) collective-permute-start(f32[12,128]{1,0:T(8,128)S(1)} %get-tuple-element.53), channel_id=1, source_target_pairs={{0,4},{4,0},{8,12},{12,8},{16,20},{20,16},{24,28},{28,24},{1,5},{5... | collective-permute-start | bytes 18440 | tf_op jit(solution)/shard_map/ppermute | solution.py:49
  25.8 1.5 %collective-permute-start.8 = (f32[12,128]{1,0:T(8,128)S(1)}, f32[12,128]{1,0:T(8,128)S(1)}, u32[]{:S(2)}, u32[]{:S(2)}) collective-permute-start(f32[12,128]{1,0:T(8,128)S(1)} %get-tuple-element.54), channel_id=1, source_target_pairs={{0,2},{2,0},{1,3},{3,1},{4,6},{6,4},{5,7},{7,5},{8,10},{10,8},{9,1... | collective-permute-start | bytes 18440 | tf_op jit(solution)/shard_map/ppermute | solution.py:49
  27.4 0.0 collective-permute-start.9
  27.4 0.0 collective-permute-done.6.refs_5_
  27.4 0.1 collective-permute-done.7.refs_6_
  27.5 2.0 %collective-permute-done.8.refs_7_ = f32[12,128]{1,0:T(8,128)S(1)} collective-permute-done((f32[12,128]{1,0:T(8,128)S(1)}, f32[12,128]{1,0:T(8,128)S(1)}, u32[]{:S(2)}, u32[]{:S(2)}) %collective-permute-start.8) | collective-permute-done | bytes 6176 | tf_op jit(solution)/shard_map/ppermute | solution.py:49
  29.5 0.0 collective-permute-done.9.refs_8_
  29.5 3.6 %shard_map.107 = (f32[16,128]{1,0:T(8,128)S(1)}, f32[8,128]{1,0:T(8,128)S(1)}, f32[8,128]{1,0:T(8,128)S(1)}, f32[8,128]{1,0:T(8,128)S(1)}, f32[8,128]{1,0:T(8,128)S(1)}) custom-call(f32[2,12,128]{2,1,0:T(8,128)S(1)} %get-tuple-element.47.refs_0_, s32[80,128]{1,0:T(8,128)S(1)} %get-tuple-element.48.refs_1_, ...), custom_call_target="tpu_custom_call" | custom-call | tf_op jit(solution)/shard_map/pallas_call | solution.py:448
  33.1 0.7 %collective-permute-start.10 = (f32[8,128]{1,0:T(8,128)S(1)}, f32[8,128]{1,0:T(8,128)S(1)}, u32[]{:S(2)}, u32[]{:S(2)}) collective-permute-start(f32[8,128]{1,0:T(8,128)S(1)} %get-tuple-element.58), channel_id=1, source_target_pairs={{4,8},{8,4},{12,16},{16,12},{20,24},{24,20},{5,9},{9,5},{13,17},{1... | collective-permute-start | bytes 12296 | tf_op jit(solution)/shard_map/ppermute | solution.py:49
  33.7 3.2 %collective-permute-start.11 = (f32[8,128]{1,0:T(8,128)S(1)}, f32[8,128]{1,0:T(8,128)S(1)}, u32[]{:S(2)}, u32[]{:S(2)}) collective-permute-start(f32[8,128]{1,0:T(8,128)S(1)} %get-tuple-element.59), channel_id=1, source_target_pairs={{0,4},{4,0},{8,12},{12,8},{16,20},{20,16},{24,28},{28,24},{1,5},{5... | collective-permute-start | bytes 12296 | tf_op jit(solution)/shard_map/ppermute | solution.py:49
  36.9 1.5 %collective-permute-start.12 = (f32[8,128]{1,0:T(8,128)S(1)}, f32[8,128]{1,0:T(8,128)S(1)}, u32[]{:S(2)}, u32[]{:S(2)}) collective-permute-start(f32[8,128]{1,0:T(8,128)S(1)} %get-tuple-element.60), channel_id=1, source_target_pairs={{0,2},{2,0},{1,3},{3,1},{4,6},{6,4},{5,7},{7,5},{8,10},{10,8},{9,1... | collective-permute-start | bytes 12296 | tf_op jit(solution)/shard_map/ppermute | solution.py:49
  38.5 0.0 collective-permute-start.13
  38.5 0.0 collective-permute-done.10.refs_3_
  38.5 0.1 collective-permute-done.11.refs_4_
  38.5 2.0 %collective-permute-done.12.refs_5_ = f32[8,128]{1,0:T(8,128)S(1)} collective-permute-done((f32[8,128]{1,0:T(8,128)S(1)}, f32[8,128]{1,0:T(8,128)S(1)}, u32[]{:S(2)}, u32[]{:S(2)}) %collective-permute-start.12) | collective-permute-done | bytes 4128 | tf_op jit(solution)/shard_map/ppermute | solution.py:49
  40.6 0.8 %shard_map.108 = f32[4,512]{1,0:T(4,128)} custom-call(f32[16,128]{1,0:T(8,128)S(1)} %get-tuple-element.56.refs_0_, s32[12,128]{1,0:T(8,128)S(1)} %get-tuple-element.45.halos_ref.refs_1_, bf16[128,1536]{1,0:T(8,128)(2,1)S(1)} %get-tuple-element.57.refs_2_, f32[8,128]{1,0:T(8,128)S(1)} %collective-permute-done.10.refs_3_, ...), custom_call_target="tpu_custom_call" | custom-call | tf_op jit(solution)/shard_map/pallas_call | solution.py:462
  (7 shorter events, 0.1 us)
Async XLA Ops:
  2.2 2.4 %collective-permute-start.2 = (f32[4,96,128]{2,1,0:T(8,128)S(1)}, f32[4,96,128]{2,1,0:T(8,128)S(1)}, u32[]{:S(2)}, u32[]{:S(2)}) collective-permute-start(f32[4,96,128]{2,1,0:T(8,128)S(1)} %get-tuple-element.35), channel_id=1, source_target_pairs={{0,1},{1,0},{2,3},{3,2},{4,5},{5,4},{6,7},{7,6},{8,9},{9,8},{10,11... | collective-permute-start | bytes 589832 | tf_op jit(solution)/shard_map/ppermute | solution.py:409
  2.7 1.2 %collective-permute-start = (f32[1,96,128]{2,1,0:T(8,128)S(1)}, f32[1,96,128]{2,1,0:T(8,128)S(1)}, u32[]{:S(2)}, u32[]{:S(2)}) collective-permute-start(f32[1,96,128]{2,1,0:T(8,128)S(1)} %get-tuple-element.33), channel_id=1, source_target_pairs={{0,1},{1,0},{2,3},{3,2},{4,5},{5,4},{6,7},{7,6},{8,9},{9,8},{10,11... | collective-permute-start | bytes 147464 | tf_op jit(solution)/shard_map/ppermute | solution.py:408
  3.9 12.5 %collective-permute-start.1 = (f32[2,96,128]{2,1,0:T(8,128)S(1)}, f32[2,96,128]{2,1,0:T(8,128)S(1)}, u32[]{:S(2)}, u32[]{:S(2)}) collective-permute-start(f32[2,96,128]{2,1,0:T(8,128)S(1)} %pad_maximum_fusion), channel_id=1, source_target_pairs={{4,8},{8,4},{12,16},{16,12},{20,24},{24,20},{5,9},{9,5},{13,17},{1... | collective-permute-start | bytes 294920 | tf_op jit(solution)/shard_map/ppermute | solution.py:411
  4.7 11.8 %collective-permute-start.5 = (f32[2,96,128]{2,1,0:T(8,128)S(1)}, f32[2,96,128]{2,1,0:T(8,128)S(1)}, u32[]{:S(2)}, u32[]{:S(2)}) collective-permute-start(f32[2,96,128]{2,1,0:T(8,128)S(1)} %pad_maximum_fusion.3), channel_id=1, source_target_pairs={{0,4},{4,0},{8,12},{12,8},{16,20},{20,16},{24,28},{28,24},{1,5},{5... | collective-permute-start | bytes 294920 | tf_op jit(solution)/shard_map/ppermute | solution.py:411
  10.3 6.1 %collective-permute-start.4 = (f32[2,96,128]{2,1,0:T(8,128)S(1)}, f32[2,96,128]{2,1,0:T(8,128)S(1)}, u32[]{:S(2)}, u32[]{:S(2)}) collective-permute-start(f32[2,96,128]{2,1,0:T(8,128)S(1)} %pad_maximum_fusion.2), channel_id=1, source_target_pairs={{8,16},{16,8},{12,20},{20,12},{9,17},{17,9},{13,21},{21,13},{10,18... | collective-permute-start | bytes 294920 | tf_op jit(solution)/shard_map/ppermute | solution.py:411
  11.0 7.1 %collective-permute-start.3 = (f32[2,96,128]{2,1,0:T(8,128)S(1)}, f32[2,96,128]{2,1,0:T(8,128)S(1)}, u32[]{:S(2)}, u32[]{:S(2)}) collective-permute-start(f32[2,96,128]{2,1,0:T(8,128)S(1)} %pad_maximum_fusion.1), channel_id=1, source_target_pairs={{0,8},{8,0},{4,12},{12,4},{16,24},{24,16},{20,28},{28,20},{1,9},{9... | collective-permute-start | bytes 294920 | tf_op jit(solution)/shard_map/ppermute | solution.py:411
  20.4 7.0 %collective-permute-start.6 = (f32[12,128]{1,0:T(8,128)S(1)}, f32[12,128]{1,0:T(8,128)S(1)}, u32[]{:S(2)}, u32[]{:S(2)}) collective-permute-start(f32[12,128]{1,0:T(8,128)S(1)} %get-tuple-element.52), channel_id=1, source_target_pairs={{4,8},{8,4},{12,16},{16,12},{20,24},{24,20},{5,9},{9,5},{13,17},{1... | collective-permute-start | bytes 18440 | tf_op jit(solution)/shard_map/ppermute | solution.py:49
  21.0 6.4 %collective-permute-start.7 = (f32[12,128]{1,0:T(8,128)S(1)}, f32[12,128]{1,0:T(8,128)S(1)}, u32[]{:S(2)}, u32[]{:S(2)}) collective-permute-start(f32[12,128]{1,0:T(8,128)S(1)} %get-tuple-element.53), channel_id=1, source_target_pairs={{0,4},{4,0},{8,12},{12,8},{16,20},{20,16},{24,28},{28,24},{1,5},{5... | collective-permute-start | bytes 18440 | tf_op jit(solution)/shard_map/ppermute | solution.py:49
  25.8 3.7 %collective-permute-start.8 = (f32[12,128]{1,0:T(8,128)S(1)}, f32[12,128]{1,0:T(8,128)S(1)}, u32[]{:S(2)}, u32[]{:S(2)}) collective-permute-start(f32[12,128]{1,0:T(8,128)S(1)} %get-tuple-element.54), channel_id=1, source_target_pairs={{0,2},{2,0},{1,3},{3,1},{4,6},{6,4},{5,7},{7,5},{8,10},{10,8},{9,1... | collective-permute-start | bytes 18440 | tf_op jit(solution)/shard_map/ppermute | solution.py:49
  27.4 2.1 %collective-permute-start.9 = (f32[12,128]{1,0:T(8,128)S(1)}, f32[12,128]{1,0:T(8,128)S(1)}, u32[]{:S(2)}, u32[]{:S(2)}) collective-permute-start(f32[12,128]{1,0:T(8,128)S(1)} %get-tuple-element.55), channel_id=1, source_target_pairs={{0,1},{1,0},{2,3},{3,2},{4,5},{5,4},{6,7},{7,6},{8,9},{9,8},{10,11... | collective-permute-start | bytes 18440 | tf_op jit(solution)/shard_map/ppermute | solution.py:49
  33.1 5.4 %collective-permute-start.10 = (f32[8,128]{1,0:T(8,128)S(1)}, f32[8,128]{1,0:T(8,128)S(1)}, u32[]{:S(2)}, u32[]{:S(2)}) collective-permute-start(f32[8,128]{1,0:T(8,128)S(1)} %get-tuple-element.58), channel_id=1, source_target_pairs={{4,8},{8,4},{12,16},{16,12},{20,24},{24,20},{5,9},{9,5},{13,17},{1... | collective-permute-start | bytes 12296 | tf_op jit(solution)/shard_map/ppermute | solution.py:49
  33.7 4.8 %collective-permute-start.11 = (f32[8,128]{1,0:T(8,128)S(1)}, f32[8,128]{1,0:T(8,128)S(1)}, u32[]{:S(2)}, u32[]{:S(2)}) collective-permute-start(f32[8,128]{1,0:T(8,128)S(1)} %get-tuple-element.59), channel_id=1, source_target_pairs={{0,4},{4,0},{8,12},{12,8},{16,20},{20,16},{24,28},{28,24},{1,5},{5... | collective-permute-start | bytes 12296 | tf_op jit(solution)/shard_map/ppermute | solution.py:49
  36.9 3.6 %collective-permute-start.12 = (f32[8,128]{1,0:T(8,128)S(1)}, f32[8,128]{1,0:T(8,128)S(1)}, u32[]{:S(2)}, u32[]{:S(2)}) collective-permute-start(f32[8,128]{1,0:T(8,128)S(1)} %get-tuple-element.60), channel_id=1, source_target_pairs={{0,2},{2,0},{1,3},{3,1},{4,6},{6,4},{5,7},{7,5},{8,10},{10,8},{9,1... | collective-permute-start | bytes 12296 | tf_op jit(solution)/shard_map/ppermute | solution.py:49
  38.5 2.1 %collective-permute-start.13 = (f32[8,128]{1,0:T(8,128)S(1)}, f32[8,128]{1,0:T(8,128)S(1)}, u32[]{:S(2)}, u32[]{:S(2)}) collective-permute-start(f32[8,128]{1,0:T(8,128)S(1)} %get-tuple-element.61), channel_id=1, source_target_pairs={{0,1},{1,0},{2,3},{3,2},{4,5},{5,4},{6,7},{7,6},{8,9},{9,8},{10,11... | collective-permute-start | bytes 12296 | tf_op jit(solution)/shard_map/ppermute | solution.py:49
